TPU v7x, 32 devices: a whole 2x2x4 slice. The times are simulated.
32 devices in a mesh: group: 2 (over x), tok: 16 (over z, y, core).
Axes of the slice: x: 2, y: 2, z: 4, core: 2. Of those that a mesh axis runs over, the one named last changes fastest.
Arguments:
- initial_guess: float32 [512, 16, 128], P(('group', 'tok')), parts along dimension 0, may hold values from -6 to 6
- noise_draws: float32 [512, 16, 128], P(('group', 'tok')), parts along dimension 0, may hold values from -6 to 6
- drift_state: float32 [16], replicated, may hold values from 0 to 0.15
- drift_denoise: float32 [16], replicated, may hold values from -0.4 to -0.15
- noise_scale: float32 [16], replicated, may hold values from 0.05 to 0.3
- modulation: float32 [16, 8, 1152], replicated, may hold values from -3 to 3
- embed_weight: bfloat16 [16, 1152], replicated, may hold values from -1.5 to 1.5
- space_input: bfloat16 [1152, 1728], replicated, may hold values from -0.1875 to 0.1875
- space_output: bfloat16 [576, 1152], replicated, may hold values from -0.25 to 0.25
- time_input: bfloat16 [1152, 1728], replicated, may hold values from -0.1875 to 0.1875
- time_output: bfloat16 [576, 1152], replicated, may hold values from -0.25 to 0.25
- final_weight: bfloat16 [1152, 16], replicated, may hold values from -0.1875 to 0.1875
Outputs:
- next_states: float32 [512, 16, 128], P(('group', 'tok')), parts along dimension 0
There are 2 independent parts, one for each index of `group`. A program takes and returns all parts, laid end to end along the dimension named above; an argument that names none is the same for every part. Nothing has to cross between parts.
All inputs are finite; a program needn't handle non-finite values.
Results may differ from a plain program's by a relative error of at most 0.006.
Values may be sent and summed in bfloat16 or wider, within the bound.
No kernel may reach another device: no remote copies, remote signals or barrier semaphores. Data moves between devices by JAX's collectives and lax.ppermute only.
A program may use at most 128 MiB of HBM per device.

v0:
```python
import jax
import jax.numpy as jnp
from jax import lax
from jax.sharding import PartitionSpec as P

HEADS = 8
HD = 72
P_SIZE = 16
ITERS = 2


def carried_in(array, axis, join, neutral):
    place = lax.axis_index(axis)
    gathered = lax.all_gather(array.astype(jnp.bfloat16), axis)
    state = jnp.zeros_like(array) + jnp.asarray(neutral, array.dtype)

    def one(hop, state):
        return join(state, lax.dynamic_index_in_dim(gathered, hop, 0, False).astype(array.dtype))

    return lax.fori_loop(0, place, one, state)


def layer_norm(values):
    center = values - jnp.mean(values, -1, keepdims=True)
    return center * lax.rsqrt(jnp.mean(center * center, -1, keepdims=True) + 1e-06)


def head_norm(values):
    return values * lax.rsqrt(jnp.mean(values * values, -1, keepdims=True) + 1e-06)


def space_mix(normed, input_weight, output_weight):
    frames, length, feature_width = normed.shape
    packed = jnp.dot(
        normed.reshape(-1, feature_width), input_weight, preferred_element_type=jnp.float32
    )
    packed = packed.reshape(frames, length, 3, HEADS, HD)
    queries = head_norm(packed[:, :, 0]).astype(jnp.bfloat16)
    key_rows = head_norm(packed[:, :, 1]).astype(jnp.bfloat16)
    value_rows = packed[:, :, 2].astype(jnp.bfloat16)

    def one_frame(triple):
        query_frame, key_frame, value_frame = triple
        scores = jnp.einsum(
            "lhe,mhe->hlm", query_frame, key_frame, preferred_element_type=jnp.float32
        ) * HD ** (-0.5)
        weights = jnp.exp(scores)
        weights = (weights / jnp.sum(weights, -1, keepdims=True)).astype(jnp.bfloat16)
        return jnp.einsum(
            "hlm,mhe->lhe", weights, value_frame, preferred_element_type=jnp.float32
        ).astype(jnp.bfloat16)

    attended = lax.map(one_frame, (queries, key_rows, value_rows))
    result = jnp.dot(
        attended.reshape(-1, HEADS * HD), output_weight, preferred_element_type=jnp.float32
    )
    return result.reshape(frames, length, feature_width)


def time_mix(normed, input_weight, output_weight):
    timesteps, groups, frames, positions, feature_width = normed.shape
    packed = jnp.dot(
        normed.reshape(-1, feature_width), input_weight, preferred_element_type=jnp.float32
    )
    packed = packed.reshape(timesteps, groups, frames, positions, 3, HEADS, HD)
    queries = head_norm(packed[:, :, :, :, 0]).astype(jnp.bfloat16)
    key_rows = head_norm(packed[:, :, :, :, 1]).astype(jnp.bfloat16)
    value_rows = packed[:, :, :, :, 2].astype(jnp.bfloat16)
    scores = jnp.einsum(
        "pglnhe,pkmnhe->pnhglkm", queries, key_rows, preferred_element_type=jnp.float32
    ) * HD ** (-0.5)
    frame_count = groups * frames
    weights = jnp.exp(scores).reshape(timesteps, positions, HEADS, frame_count, frame_count)
    weights = (weights / jnp.sum(weights, -1, keepdims=True)).astype(jnp.bfloat16)
    weights = weights.reshape(timesteps, positions, HEADS, groups, frames, groups, frames)
    attended = jnp.einsum(
        "pnhglkm,pkmnhe->pglnhe", weights, value_rows, preferred_element_type=jnp.float32
    ).astype(jnp.bfloat16)
    result = jnp.dot(
        attended.reshape(-1, HEADS * HD), output_weight, preferred_element_type=jnp.float32
    )
    return result.reshape(timesteps, groups, frames, positions, feature_width)


def body(
    initial_guess,
    noise_draws,
    drift_state,
    drift_denoise,
    noise_scale,
    modulation,
    embed_weight,
    space_input,
    space_output,
    time_input,
    time_output,
    final_weight,
):
    frames_local, channels, spatial = initial_guess.shape
    model_width = embed_weight.shape[1]
    devices = lax.axis_size("tok")
    own_index = lax.axis_index("tok")
    groups = devices // P_SIZE
    timestep = own_index // groups
    block_index = own_index % groups
    positions = spatial // devices
    leading = timestep == 0
    modulation_row = lax.dynamic_index_in_dim(modulation, timestep, 0, keepdims=False)
    time_table = modulation.reshape(P_SIZE, 1, 1, 1, 8, model_width)
    rate_state = lax.dynamic_index_in_dim(drift_state, timestep, 0, keepdims=False)
    rate_denoise = lax.dynamic_index_in_dim(drift_denoise, timestep, 0, keepdims=False)
    rate_noise = lax.dynamic_index_in_dim(noise_scale, timestep, 0, keepdims=False)
    latent = initial_guess
    result = initial_guess
    for iteration in range(ITERS):
        embedded = jnp.einsum(
            "fch,cd->fhd",
            latent.astype(jnp.bfloat16),
            embed_weight,
            preferred_element_type=jnp.float32,
        )
        normed = (layer_norm(embedded) * (1.0 + modulation_row[1]) + modulation_row[0]).astype(
            jnp.bfloat16
        )
        after_space = (
            embedded + modulation_row[2] * space_mix(normed, space_input, space_output)
        ).astype(jnp.bfloat16)
        temporal = lax.all_to_all(after_space, "tok", split_axis=1, concat_axis=0, tiled=True)
        hidden = temporal.reshape(P_SIZE, groups, frames_local, positions, model_width).astype(
            jnp.float32
        )
        normed = (
            layer_norm(hidden) * (1.0 + time_table[:, :, :, :, 4]) + time_table[:, :, :, :, 3]
        ).astype(jnp.bfloat16)
        after_time = (
            hidden + time_table[:, :, :, :, 5] * time_mix(normed, time_input, time_output)
        ).astype(jnp.bfloat16)
        settled = lax.optimization_barrier(after_time).astype(jnp.float32)
        normed = (
            layer_norm(settled) * (1.0 + time_table[:, :, :, :, 7]) + time_table[:, :, :, :, 6]
        ).astype(jnp.bfloat16)
        outgoing = jnp.einsum(
            "pglnd,dc->pglcn", normed, final_weight, preferred_element_type=jnp.float32
        )
        outgoing = outgoing.reshape(devices * frames_local, channels, positions)
        predicted = lax.all_to_all(outgoing, "tok", split_axis=0, concat_axis=2, tiled=True)
        increment = rate_state * latent + rate_denoise * predicted + rate_noise * noise_draws
        increment = jnp.where(leading, increment + latent, increment)

        def combine(first_part, second_part):
            return first_part + second_part

        slot_mask = (jnp.arange(groups, dtype=jnp.int32) == block_index).astype(jnp.float32)
        slotted = slot_mask[:, None, None, None] * increment[None]
        scanned = carried_in(slotted, "tok", combine, jnp.zeros_like(slotted))
        before = lax.dynamic_index_in_dim(scanned, block_index, 0, keepdims=False)
        result = jnp.where(leading, 0.0, before) + increment
        latent = jnp.where(leading, latent, before)
    return result


def solution(mesh):
    placed = (
        P(("group", "tok"), None, None),
        P(("group", "tok"), None, None),
        P(),
        P(),
        P(),
        P(),
        P(),
        P(),
        P(),
        P(),
        P(),
        P(),
    )
    return jax.shard_map(
        body, mesh=mesh, in_specs=placed, out_specs=P(("group", "tok"), None, None), check_vma=False
    )
```

profile of v0, /device:TPU:29, one launch (start us, length us, event | category | flops | bytes accessed | tf_op | source)
XLA Modules:
  0.0 738.1 jit_solution(5119831308410877056)
XLA Ops:
  6.5 2.5 fusion.135
  10.2 2.5 copy-done.1
  13.3 14.4 %fusion.65 = f32[16,128,3,8,72]{1,4,3,2,0:T(8,128)S(1)} fusion(bf16[3,8,72,1152,1]{3,2,1,0,4:T(8,128)(2,1)} %bitcast.338, f32[16,128,1152]{2,1,0:T(8,128)} %copy-done.1, f32[1152]{0:T(1024)S(1)} %get-tuple-element.175, f32[1152]{0:T(1024)S(1)} %get-tuple-element.174, f32[16,128]{1,0:T(8,128)S(1)} %add_rsqrt_fusion.13, ...), kind=kOutput, calls=%fused_computation.97 | convolution fusion | flops 8165523456 | bytes 27599872 | tf_op jit(solution)/shard_map/dot_general | solution.py:34
  29.4 3.3 copy-done.4
  32.8 1.9 fusion.116
  34.7 7.6 %multiply_convert_fusion.2 = (bf16[16,128,8,72]{1,3,2,0:T(8,128)(2,1)}, bf16[16,128,8,72]{1,3,2,0:T(8,128)(2,1)}) fusion(f32[16,128,3,8,72]{1,4,3,2,0:T(8,128)} %copy-done.4, f32[16,128,8]{1,2,0:T(8,128)S(1)} %get-tuple-element.235, f32[16,128,8]{1,2,0:T(8,128)S(1)} %get-tuple-element.236), kind=kLoop, calls=%fused_computation.126 | loop fusion | flops 4718592 | bytes 14286848 | tf_op jit(solution)/shard_map/convert_element_type | solution.py:39
  42.2 1.9 broadcast.316.clone
  44.1 49.8 %while.40 = (s32[]{:T(128)}, bf16[16,128,8,72]{1,3,2,0:T(8,128)(2,1)}, bf16[16,128,8,72]{1,3,2,0:T(8,128)(2,1)}, bf16[16,128,8,72]{1,3,2,0:T(8,128)(2,1)}, bf16[16,128,8,72]{1,3,2,0:T(8,128)(2,1)}, /*index=5*/s32[]{:T(128)}) while((s32[]{:T(128)}, bf16[16,128,8,72]{1,3,2,0:T(8,128)(2,1)}, bf16[16,128,8,72]{1,3,2,0:T(8,128)(2,1)}, ...), condition=%wide.region_6.7_spmd, body=%wide.region_4.6_spmd.sunk | while | flops 38216832 | bytes 2164805 | solution.py:53
  51.6 1.9 fusion.164
  70.3 1.8 fusion.164
  73.4 1.8 fusion.164
  85.8 1.8 fusion.164
  88.9 1.8 fusion.164
  93.9 8.0 %add_convert_fusion.4 = bf16[16,128,1152]{2,1,0:T(8,128)(2,1)S(1)} fusion(f32[16,128,1152]{2,1,0:T(8,128)} %copy-done.1, bf16[16,128,576]{1,2,0:T(8,128)(2,1)} %bitcast.324, f32[1152]{0:T(1024)S(1)} %get-tuple-element.173, bf16[576,1152]{1,0:T(8,128)(2,1)S(1)} %copy-done), kind=kOutput, calls=%fused_computation.71 | convolution fusion | flops 2724986880 | bytes 17846784 | tf_op jit(solution)/shard_map/dot_general | solution.py:54
  101.9 4.8 copy.200
  106.7 6.6 all-to-all-start
  113.7 102.2 %all-to-all-done = bf16[16,128,1152]{2,0,1:T(8,128)(2,1)} async-done(((bf16[16,128,1152]{2,0,1:T(8,128)(2,1)}), bf16[16,128,1152]{2,0,1:T(8,128)(2,1)}, u32[]{:S(2)}, u32[]{:S(2)}) %all-to-all-start) | async-done | bytes 4718624 | tf_op jit(solution)/shard_map/all_to_all | solution.py:128
  215.9 3.2 bitcast_reduce_fusion.1
  219.2 3.8 multiply_reduce_fusion.2
  223.0 22.4 %convolution_bitcast_fusion.1 = f32[16,1,16,8,3,8,72]{6,3,5,4,2,0,1:T(8,128)} fusion(bf16[3,8,72,1152,1,1]{3,2,1,0,5,4:T(8,128)(2,1)S(1)} %bitcast.340, f32[16,1152]{1,0:T(8,128)S(1)} %get-tuple-element.239, f32[16,1152]{1,0:T(8,128)S(1)} %get-tuple-element.240, f32[16,16,8]{2,1,0:T(8,128)S(1)} %add_rsqrt_fusion.7, ...), kind=kOutput, calls=%fused_computation.75 | convolution fusion | flops 8167882752 | bytes 23019520 | tf_op jit(solution)/shard_map/dot_general | solution.py:62
  245.4 8.6 %multiply_reduce_fusion.7 = (f32[16,16,8,8]{2,3,1,0:T(8,128)S(1)}, f32[16,16,8,8]{2,3,1,0:T(8,128)S(1)}) fusion(f32[16,1,16,8,3,8,72]{6,3,5,4,2,0,1:T(8,128)} %convolution_bitcast_fusion.1), kind=kLoop, calls=%fused_computation.93 | loop fusion | flops 4685824 | bytes 9568256 | tf_op jit(solution)/shard_map/reduce_sum | solution.py:29
  254.0 4.5 fusion.98
  258.8 7.5 %fusion.61 = (bf16[16,16,8,8,72]{4,2,3,1,0:T(8,128)(2,1)S(1)}, bf16[16,16,8,8,72]{4,2,3,1,0:T(8,128)(2,1)S(1)}) fusion(f32[16,1,16,8,3,8,72]{6,3,5,4,2,0,1:T(8,128)} %convolution_bitcast_fusion.1, f32[16,16,8,8]{2,3,1,0:T(8,128)S(1)} %add_rsqrt_fusion.3, f32[16,16,8,8]{2,3,1,0:T(8,128)S(1)} %add_rsqrt_fusion.2), kind=kLoop, calls=%fused_computation.85 | loop fusion | flops 4718592 | bytes 14286848 | tf_op jit(solution)/shard_map/convert_element_type | solution.py:66
  266.3 11.6 %fusion.62 = (f32[16,8,8,16]{3,2,1,0:T(8,128)S(1)}, f32[16,8,8,16,16]{3,4,2,1,0:T(8,128)}) fusion(bf16[16,16,8,8,72]{4,2,3,1,0:T(8,128)(2,1)S(1)} %get-tuple-element.217, bf16[16,16,8,8,72]{4,2,3,1,0:T(8,128)(2,1)S(1)} %get-tuple-element.216), kind=kOutput, calls=%fused_computation.94 | convolution fusion | flops 38256640 | bytes 5832704 | tf_op jit(solution)/shard_map/pglnhe,pkmnhe->pnhglkm/dot_general | solution.py:69
  278.0 6.0 convert_bitcast_fusion.1
  284.0 3.0 copy.207
  287.0 7.4 %dot_general.100 = bf16[16,16,8,576]{3,2,1,0:T(8,128)(2,1)} reshape(bf16[16,1,16,8,8,72]{5,4,3,2,0,1:T(8,128)(2,1)} %copy.207) | data formatting | bytes 4718592 | tf_op jit(solution)/shard_map/dot_general | solution.py:79
  294.4 8.2 %fusion.96 = bf16[16,1,16,8,1152]{4,3,2,0,1:T(8,128)(2,1)S(1)} fusion(bf16[16,16,8,576]{3,2,1,0:T(8,128)(2,1)} %dot_general.100, f32[16,1152]{1,0:T(8,128)S(1)} %bitcast.336, bf16[576,1152]{1,0:T(8,128)(2,1)S(1)} %copy-done.26, bf16[16,128,1152]{2,0,1:T(8,128)(2,1)} %all-to-all-done), kind=kOutput, calls=%fused_computation.138 | convolution fusion | flops 2727346176 | bytes 13197312 | tf_op jit(solution)/shard_map/dot_general | solution.py:79
  304.8 1.9 fusion.94
  307.8 5.9 all-to-all-start.1
  315.7 2.2 all-to-all-done.1
  322.7 2.9 fusion.122
  325.6 37.1 %all-gather.5.cloned.1.call-done = bf16[256,16,128]{2,1,0:T(8,128)(2,1)} async-done(((bf16[16,16,128]{2,1,0:T(8,128)(2,1)}), bf16[256,16,128]{2,1,0:T(8,128)(2,1)}) %all-gather.5.cloned.1.call-update) | async-done | bytes 1048592 | tf_op jit(solution)/shard_map/all_gather | solution.py:14
  362.7 13.4 %while.41 = (s32[]{:T(128)}, f32[1,16,16,128]{3,2,1,0:T(8,128)S(1)}, s32[]{:T(128)}, bf16[16,1,16,16,128]{4,3,2,1,0:T(8,128)(2,1)}, s32[]{:T(128)}, /*index=5*/s32[]{:T(128)}, s32[]{:T(128)}) while((s32[]{:T(128)}, f32[1,16,16,128]{3,2,1,0:T(8,128)S(1)}, s32[]{:T(128)}, bf16[16,1,16,16,128]{4,3,2,1,0:T(8,128)(2,1)}, s32[]{:T(128)}, ...), condition=%wide.region_15.16_spmd, body=%wide.region_14.15_spmd.sunk | while | flops 65541 | bytes 327795 | solution.py:20
  376.2 2.3 fusion.136
  379.6 2.5 copy-done.2
  382.1 11.6 %fusion.70 = f32[16,128,3,8,72]{1,4,3,2,0:T(8,128)S(1)} fusion(bf16[3,8,72,1152,1]{3,2,1,0,4:T(8,128)(2,1)} %bitcast.339, f32[16,128,1152]{2,1,0:T(8,128)S(1)} %get-tuple-element.232, f32[16,128]{1,0:T(8,128)S(1)} %add_rsqrt_fusion.12, f32[16,128]{1,0:T(8,128)S(1)} %broadcast_multiply_fusion.6, f32[1152]{0:T(1024)S(1)} %copy-done.23, f32[1152]{0:T(1024)S(1)} %copy-done.21), kind=kOutput, calls=%fused_computation.100 | convolution fusion | flops 8165523456 | bytes 27599872 | tf_op jit(solution)/shard_map/dot_general | solution.py:34
  397.2 3.4 multiply_convert_fusion
  400.6 1.9 broadcast.316
  402.5 49.8 %while.42 = (s32[]{:T(128)}, bf16[16,128,8,72]{1,3,2,0:T(8,128)(2,1)}, bf16[16,128,8,72]{1,3,2,0:T(8,128)(2,1)}, bf16[16,128,8,72]{1,3,2,0:T(8,128)(2,1)}, bf16[16,128,8,72]{1,3,2,0:T(8,128)(2,1)}, /*index=5*/s32[]{:T(128)}) while((s32[]{:T(128)}, bf16[16,128,8,72]{1,3,2,0:T(8,128)(2,1)}, bf16[16,128,8,72]{1,3,2,0:T(8,128)(2,1)}, ...), condition=%wide.region_22.23_spmd, body=%wide.region_20.22_spmd.sunk | while | flops 38216832 | bytes 2164805 | solution.py:53
  406.9 1.8 fusion.170
  410.0 1.8 fusion.170
  413.1 1.8 fusion.170
  434.9 1.8 fusion.170
  438.0 1.9 fusion.170
  450.4 1.8 fusion.170
  452.3 8.2 %add_convert_fusion.1 = bf16[16,128,1152]{2,1,0:T(8,128)(2,1)S(1)} fusion(f32[16,128,1152]{2,1,0:T(8,128)} %copy-done.2, bf16[16,128,576]{1,2,0:T(8,128)(2,1)} %bitcast.323, f32[1152]{0:T(1024)S(1)} %copy-done.9, bf16[576,1152]{1,0:T(8,128)(2,1)S(1)} %copy-done), kind=kOutput, calls=%fused_computation.66 | convolution fusion | flops 2724986880 | bytes 17846784 | tf_op jit(solution)/shard_map/dot_general | solution.py:54
  460.5 2.7 copy.212
  463.2 108.5 %all_to_all.16 = bf16[16,128,1152]{2,0,1:T(8,128)(2,1)S(1)} all-to-all(bf16[16,128,1152]{2,0,1:T(8,128)(2,1)S(1)} %copy.212), channel_id=1, replica_groups=mesh['group'=2,'tok'=16] {'tok'}, dimensions={1} | all-to-all | bytes 9437184 | tf_op jit(solution)/shard_map/all_to_all | solution.py:128
  575.6 19.9 %convolution_bitcast_fusion = f32[16,1,16,8,3,8,72]{6,3,5,4,2,0,1:T(8,128)} fusion(bf16[3,8,72,1152,1,1]{3,2,1,0,5,4:T(8,128)(2,1)S(1)} %bitcast.341, f32[16,16,8]{2,1,0:T(8,128)S(1)} %add_rsqrt_fusion.5, f32[16,16,8]{2,1,0:T(8,128)S(1)} %broadcast_multiply_fusion.1, f32[16,1152]{1,0:T(8,128)S(1)} %copy-done.17, f32[16,1152]{1,0:T(8,128)S(1)} %copy-done.19, ...), kind=kOutput, calls=%fused_computation.74 | convolution fusion | flops 8167882752 | bytes 23019520 | tf_op jit(solution)/shard_map/dot_general | solution.py:62
  595.5 8.6 %multiply_reduce_fusion.5 = (f32[16,16,8,8]{2,3,1,0:T(8,128)S(1)}, f32[16,16,8,8]{2,3,1,0:T(8,128)S(1)}) fusion(f32[16,1,16,8,3,8,72]{6,3,5,4,2,0,1:T(8,128)} %convolution_bitcast_fusion), kind=kLoop, calls=%fused_computation.89 | loop fusion | flops 4685824 | bytes 9568256 | tf_op jit(solution)/shard_map/reduce_sum | solution.py:29
  604.0 6.5 fusion.99
  610.8 7.5 %fusion.59 = (bf16[16,16,8,8,72]{4,2,3,1,0:T(8,128)(2,1)S(1)}, bf16[16,16,8,8,72]{4,2,3,1,0:T(8,128)(2,1)S(1)}) fusion(f32[16,1,16,8,3,8,72]{6,3,5,4,2,0,1:T(8,128)} %convolution_bitcast_fusion, f32[16,16,8,8]{2,3,1,0:T(8,128)S(1)} %add_rsqrt_fusion.1, f32[16,16,8,8]{2,3,1,0:T(8,128)S(1)} %add_rsqrt_fusion), kind=kLoop, calls=%fused_computation.81 | loop fusion | flops 4718592 | bytes 14286848 | tf_op jit(solution)/shard_map/convert_element_type | solution.py:66
  618.3 11.8 %fusion.63 = (f32[16,8,8,16]{3,2,1,0:T(8,128)S(1)}, f32[16,8,8,16,16]{3,4,2,1,0:T(8,128)}) fusion(bf16[16,16,8,8,72]{4,2,3,1,0:T(8,128)(2,1)S(1)} %get-tuple-element.215, bf16[16,16,8,8,72]{4,2,3,1,0:T(8,128)(2,1)S(1)} %get-tuple-element.214), kind=kOutput, calls=%fused_computation.95 | convolution fusion | flops 38256640 | bytes 5832704 | tf_op jit(solution)/shard_map/pglnhe,pkmnhe->pnhglkm/dot_general | solution.py:69
  630.2 8.6 %convert_bitcast_fusion = bf16[16,1,16,8,8,72]{5,2,4,3,0,1:T(8,128)(2,1)S(1)} fusion(f32[16,8,8,16,16]{3,4,2,1,0:T(8,128)} %get-tuple-element.234, f32[16,8,8,16]{3,2,1,0:T(8,128)S(1)} %get-tuple-element.233, bf16[16,16,8,8,72]{4,2,3,1,0:T(8,128)(2,1)} %fusion.99), kind=kOutput, calls=%fused_computation.152 | convolution fusion | flops 39714816 | bytes 5832704 | tf_op jit(solution)/shard_map/pnhglkm,pkmnhe->pglnhe/dot_general | solution.py:76
  638.8 3.0 copy.219
  641.8 7.4 %dot_general.113 = bf16[16,16,8,576]{3,2,1,0:T(8,128)(2,1)} reshape(bf16[16,1,16,8,8,72]{5,4,3,2,0,1:T(8,128)(2,1)} %copy.219) | data formatting | bytes 4718592 | tf_op jit(solution)/shard_map/dot_general | solution.py:79
  649.2 7.9 %fusion.97 = bf16[16,1,16,8,1152]{4,3,2,0,1:T(8,128)(2,1)S(1)} fusion(bf16[16,16,8,576]{3,2,1,0:T(8,128)(2,1)} %dot_general.113, f32[16,1152]{1,0:T(8,128)S(1)} %bitcast.337, bf16[576,1152]{1,0:T(8,128)(2,1)S(1)} %copy-done.27, bf16[16,128,1152]{2,0,1:T(8,128)(2,1)} %copy-done.3), kind=kOutput, calls=%fused_computation.139 | convolution fusion | flops 2727346176 | bytes 13197312 | tf_op jit(solution)/shard_map/dot_general | solution.py:79
  659.4 1.9 fusion.92
  661.6 9.9 %all_to_all.17 = f32[16,1,2048]{2,1,0:T(1,128)S(1)} all-to-all(f32[16,1,2048]{2,1,0:T(1,128)S(1)} %reshape.508), channel_id=1, replica_groups=mesh['group'=2,'tok'=16] {'tok'}, dimensions={0} | all-to-all | bytes 262144 | tf_op jit(solution)/shard_map/all_to_all | solution.py:146
  674.3 2.0 copy.221
  677.8 2.0 fusion.134
  679.8 37.2 %all-gather.7.cloned.1.call-done = bf16[256,16,128]{2,1,0:T(8,128)(2,1)} async-done(((bf16[16,16,128]{2,1,0:T(8,128)(2,1)}), bf16[256,16,128]{2,1,0:T(8,128)(2,1)}) %all-gather.7.cloned.1.call-update) | async-done | bytes 1048592 | tf_op jit(solution)/shard_map/all_gather | solution.py:14
  717.0 13.4 %while.43 = (s32[]{:T(128)}, f32[1,16,16,128]{3,2,1,0:T(8,128)S(1)}, s32[]{:T(128)}, bf16[16,1,16,16,128]{4,3,2,1,0:T(8,128)(2,1)}, s32[]{:T(128)}, /*index=5*/s32[]{:T(128)}, s32[]{:T(128)}) while((s32[]{:T(128)}, f32[1,16,16,128]{3,2,1,0:T(8,128)S(1)}, s32[]{:T(128)}, bf16[16,1,16,16,128]{4,3,2,1,0:T(8,128)(2,1)}, s32[]{:T(128)}, ...), condition=%wide.region_31.32_spmd, body=%wide.region_30.31_spmd.sunk | while | flops 65541 | bytes 327795 | solution.py:20
  (207 shorter events, 135.3 us)
Async XLA Ops:
  6.5 87.4 %copy-start = (bf16[576,1152]{1,0:T(8,128)(2,1)S(1)}, bf16[576,1152]{1,0:T(8,128)(2,1)}, u32[]{:S(2)}) copy-start(bf16[576,1152]{1,0:T(8,128)(2,1)} %param.28) | copy-start | bytes 3981316
  9.1 3.6 copy-start.1
  9.1 3.6 copy-start.7
  12.7 0.6 copy-start.20
  12.7 0.6 copy-start.22
  12.7 81.2 %copy-start.8 = (f32[1152]{0:T(1024)}, f32[1152]{0:T(1024)S(1)}, u32[]{:S(2)}) copy-start(f32[1152]{0:T(1024)S(1)} %get-tuple-element.173) | copy-start | bytes 13828
  27.7 5.1 copy-start.4
  106.7 109.2 %all-to-all-start = ((bf16[16,128,1152]{2,0,1:T(8,128)(2,1)}), bf16[16,128,1152]{2,0,1:T(8,128)(2,1)}, u32[]{:S(2)}, u32[]{:S(2)}) async-start(bf16[16,128,1152]{2,0,1:T(8,128)(2,1)} %copy.200), calls=%async_computation | async-start | bytes 9437184 | tf_op jit(solution)/shard_map/all_to_all | solution.py:128
  113.7 180.8 %copy-start.10 = (f32[16,1,1,1,1,1152]{5,0,4,3,2,1:T(8,128)}, f32[16,1,1,1,1,1152]{5,0,4,3,2,1:T(8,128)S(1)}, u32[]{:S(2)}) copy-start(f32[16,1,1,1,1,1152]{5,0,4,3,2,1:T(8,128)S(1)} %copy.299) | copy-start | bytes 221188
  113.7 109.3 %copy-start.16 = (f32[16,1152]{1,0:T(8,128)}, f32[16,1152]{1,0:T(8,128)S(1)}, u32[]{:S(2)}) copy-start(f32[16,1152]{1,0:T(8,128)S(1)} %get-tuple-element.239) | copy-start | bytes 221188
  113.7 109.3 %copy-start.18 = (f32[16,1152]{1,0:T(8,128)}, f32[16,1152]{1,0:T(8,128)S(1)}, u32[]{:S(2)}) copy-start(f32[16,1152]{1,0:T(8,128)S(1)} %get-tuple-element.240) | copy-start | bytes 221188
  113.7 191.0 %copy-start.12 = (f32[16,1152]{1,0:T(8,128)}, f32[16,1152]{1,0:T(8,128)S(1)}, u32[]{:S(2)}) copy-start(f32[16,1152]{1,0:T(8,128)S(1)} %get-tuple-element.237) | copy-start | bytes 221188
  113.7 191.0 %copy-start.14 = (f32[16,1152]{1,0:T(8,128)}, f32[16,1152]{1,0:T(8,128)S(1)}, u32[]{:S(2)}) copy-start(f32[16,1152]{1,0:T(8,128)S(1)} %get-tuple-element.238) | copy-start | bytes 221188
  215.9 7.1 copy-start.24
  287.0 7.4 %copy-start.26 = (bf16[576,1152]{1,0:T(8,128)(2,1)S(1)}, bf16[576,1152]{1,0:T(8,128)(2,1)}, u32[]{:S(2)}) copy-start(bf16[576,1152]{1,0:T(8,128)(2,1)} %param.30) | copy-start | bytes 3981316
  302.6 2.2 copy-start.28
  304.8 8.9 %copy-start.30 = (f32[16]{0:T(128)S(1)}, f32[16]{0:T(128)}, u32[]{:S(2)}) copy-start(f32[16]{0:T(128)} %param.23) | copy-start | bytes 196
  304.8 9.6 %copy-start.31 = (f32[16]{0:T(128)S(1)}, f32[16]{0:T(128)}, u32[]{:S(2)}) copy-start(f32[16]{0:T(128)} %param.22) | copy-start | bytes 196
  304.8 10.2 %copy-start.32 = (f32[16]{0:T(128)S(1)}, f32[16]{0:T(128)}, u32[]{:S(2)}) copy-start(f32[16]{0:T(128)} %param.24) | copy-start | bytes 196
  306.7 15.9 %copy-start.5 = (f32[16,16,128]{2,1,0:T(8,128)S(1)}, f32[16,16,128]{2,1,0:T(8,128)}, u32[]{:S(2)}) copy-start(f32[16,16,128]{2,1,0:T(8,128)} %param.20) | copy-start | bytes 393220
  307.8 10.1 %all-to-all-start.1 = ((f32[16,1,2048]{2,1,0:T(1,128)}), f32[16,1,2048]{2,1,0:T(1,128)S(1)}, u32[]{:S(2)}, u32[]{:S(2)}) async-start(f32[16,1,2048]{2,1,0:T(1,128)} %reshape.506), calls=%async_computation.1 | async-start | bytes 262144 | tf_op jit(solution)/shard_map/all_to_all | solution.py:146
  313.7 49.1 %all-gather.5.cloned.1.call-start = ((), (), s32[]{:S(2)}) async-start(), calls=%async_computation.4 | async-start | bytes 1114112 | tf_op jit(solution)/shard_map/all_gather | solution.py:14
  325.5 391.4 %all-gather.7.cloned.1.call-start = ((), (), s32[]{:S(2)}) async-start(), calls=%async_computation.5 | async-start | bytes 1114112 | tf_op jit(solution)/shard_map/all_gather | solution.py:14
  378.4 3.6 copy-start.2
  378.5 3.6 copy-start.21
  378.5 3.6 copy-start.23
  402.5 49.8 %copy-start.9 = (f32[1152]{0:T(1024)S(1)}, f32[1152]{0:T(1024)}, u32[]{:S(2)}) copy-start(f32[1152]{0:T(1024)} %copy-done.8) | copy-start | bytes 13828
  571.7 2.6 copy-start.3
  571.7 2.6 copy-start.17
  571.7 2.6 copy-start.19
  571.7 3.9 copy-start.25
  641.8 7.4 %copy-start.11 = (f32[16,1,1,1,1,1152]{5,0,4,3,2,1:T(8,128)S(1)}, f32[16,1,1,1,1,1152]{5,0,4,3,2,1:T(8,128)}, u32[]{:S(2)}) copy-start(f32[16,1,1,1,1,1152]{5,0,4,3,2,1:T(8,128)} %copy-done.10) | copy-start | bytes 221188
  641.8 7.4 %copy-start.27 = (bf16[576,1152]{1,0:T(8,128)(2,1)S(1)}, bf16[576,1152]{1,0:T(8,128)(2,1)}, u32[]{:S(2)}) copy-start(bf16[576,1152]{1,0:T(8,128)(2,1)} %param.30) | copy-start | bytes 3981316
  657.1 2.2 copy-start.13
  657.1 2.2 copy-start.15
  657.2 2.2 copy-start.29
  661.2 16.6 %copy-start.6 = (f32[16,16,128]{2,1,0:T(8,128)S(1)}, f32[16,16,128]{2,1,0:T(8,128)}, u32[]{:S(2)}) copy-start(f32[16,16,128]{2,1,0:T(8,128)} %param.21) | copy-start | bytes 393220
Sparse Core Ops, SparseCore 0:
  325.7 37.0 all-gather.4
  680.0 36.9 all-gather.6
where the time goes:
time: 744 us; the launch traced here: 738 us
  matrix products  247 us (33%)
  waiting for transfers between devices  179 us (24%)
  blocking collectives  118 us (16%)
  other arithmetic  98.4 us (13%)
  local copies, waits for them, and re-layouts  68 us (9%)
  between operations  14.3 us (2%)
  starting transfers between devices  12.6 us (2%)
    all_to_all x1, blocking collectives, body(): lax.all_to_all(after_space, 'tok', split_axis=1, concat_axis=0, tiled=True)  109 us
    all_to_all x1, waiting for transfers between devices, body(): lax.all_to_all(after_space, 'tok', split_axis=1, concat_axis=0, tiled=True)  102 us
    all_gather x2, waiting for transfers between devices, carried_in(): gathered = lax.all_gather(array.astype(jnp.bfloat16), axis)  74.3 us
    dot_general x32, matrix products, one_frame(): jnp.einsum('hlm,mhe->lhe', weights, value_frame, preferred_element_type=j...  58.8 us
    dot_general x2, matrix products, time_mix(): jnp.dot(normed.reshape(-1, feature_width), input_weight, preferred_elemen...  42.2 us
    dot_general x32, matrix products, one_frame(): jnp.einsum('lhe,mhe->hlm', query_frame, key_frame, preferred_element_type...  40.5 us
    dot_general x2, matrix products, space_mix(): jnp.dot(normed.reshape(-1, feature_width), input_weight, preferred_elemen...  26 us
    add x30, other arithmetic, combine(): return first_part + second_part  26 us
  transfers between devices with their start and end apart: 4, of which 4 were waited for; matrix products, arithmetic and copies ran while one was open for 0% of the time, Pallas kernels for 0%

commit v1 on v0

v1 whole, which is shorter than its diff:
```python
import functools
import math

import jax
import jax.numpy as jnp
from jax import lax
from jax.experimental import pallas as pl
from jax.experimental.pallas import tpu as pltpu
from jax.sharding import PartitionSpec as P

HEADS = 8
ITERS = 2
LANES = 128
ROWS8 = 8
F32 = jnp.float32
BF16 = jnp.bfloat16


def layer_norm(values):
    center = values - jnp.mean(values, -1, keepdims=True)
    return center * lax.rsqrt(jnp.mean(center * center, -1, keepdims=True) + 1e-06)


def head_spans(lane_start, lanes, head_size):
    spans = []
    for head in range(HEADS):
        first = max(head * head_size, lane_start) - lane_start
        last = min((head + 1) * head_size, lane_start + lanes) - lane_start
        if first < last:
            spans.append((head, first, last))
    return spans


def lane_mask(shape, first, last):
    lanes = lax.broadcasted_iota(jnp.int32, shape, len(shape) - 1)
    return (lanes >= first) & (lanes < last)


def normed_heads(values, head_size, scale):
    rows, width = values.shape
    tiles = [values[:, at : at + LANES] for at in range(0, width, LANES)]
    totals = [None] * HEADS
    for index, tile in enumerate(tiles):
        square = tile * tile
        for head, first, last in head_spans(index * LANES, LANES, head_size):
            part = jnp.where(lane_mask((1, LANES), first, last), square, 0.0)
            totals[head] = part if totals[head] is None else totals[head] + part
    rates = [
        lax.rsqrt(jnp.sum(total, -1, keepdims=True) * (1.0 / head_size) + 1e-06) * scale
        for total in totals
    ]
    normed = []
    for index, tile in enumerate(tiles):
        spans = head_spans(index * LANES, LANES, head_size)
        rate = rates[spans[-1][0]]
        for head, first, last in reversed(spans[:-1]):
            rate = jnp.where(lane_mask((1, LANES), 0, last), rates[head], rate)
        normed.append((tile * rate).astype(BF16))
    return normed


def attention(normed, input_weight, output_weight, group_rows, same_position):
    rows = normed.shape[0]
    inner = output_weight.shape[0]
    head_size = inner // HEADS
    wide = -(-inner // LANES) * LANES
    packed = jnp.dot(normed, input_weight, preferred_element_type=F32)
    queries = normed_heads(
        packed[:, :wide], head_size, head_size ** (-0.5) * math.log2(math.e)
    )
    key_rows = normed_heads(packed[:, inner : inner + wide], head_size, 1.0)
    value_rows = packed[:, 2 * inner :].astype(BF16)
    attended_groups = []
    for start in range(0, rows, group_rows):
        stop = start + group_rows
        attended = [None] * (wide // LANES)
        for pair in range(HEADS // 2):
            base = 2 * pair * head_size // LANES
            tiles = [base, base + 1]
            keys = jnp.concatenate([key_rows[t][start:stop] for t in tiles], 1)
            window = jnp.concatenate([queries[t][start:stop] for t in tiles], 1)
            low = base * LANES
            high = min(low + 2 * LANES, inner)
            values = value_rows[start:stop, low:high]
            weights, stacked, rates = [], [], []
            for head in (2 * pair, 2 * pair + 1):
                first, last = head * head_size - low, (head + 1) * head_size - low
                query = jnp.where(
                    lane_mask((1, 2 * LANES), first, last), window, jnp.zeros_like(window)
                )
                scores = lax.dot_general(
                    query, keys, (((1,), (1,)), ((), ())), preferred_element_type=F32
                )
                weight = jnp.exp2(scores)
                if same_position is not None:
                    weight = weight * same_position
                rates.append(1.0 / jnp.sum(weight, -1, keepdims=True))
                weights.append(weight.astype(BF16))
                stacked.append(
                    jnp.where(
                        lane_mask((1, high - low), first, last), values, jnp.zeros_like(values)
                    )
                )
            mixed = jnp.dot(
                jnp.concatenate(weights, 1),
                jnp.concatenate(stacked, 0),
                preferred_element_type=F32,
            )
            border = (2 * pair + 1) * head_size - low
            mixed = mixed * jnp.where(
                lane_mask((1, high - low), 0, border), rates[0], rates[1]
            )
            for t in tiles:
                at = t * LANES - low
                part = mixed[:, at : min(at + LANES, high - low)]
                attended[t] = part if attended[t] is None else attended[t] + part
        attended_groups.append(
            jnp.concatenate([part.astype(BF16) for part in attended], 1)
        )
    attended = (
        jnp.concatenate(attended_groups, 0) if len(attended_groups) > 1 else attended_groups[0]
    )
    return jnp.dot(attended, output_weight, preferred_element_type=F32)


def space_step(at, frames, latent, embed, rows_of, input_weight, output_weight, out):
    spatial = latent.shape[2]
    embedded = jnp.concatenate(
        [
            lax.dot_general(
                latent[at + index].astype(BF16),
                embed[...],
                (((0,), (0,)), ((), ())),
                preferred_element_type=F32,
            )
            for index in range(frames)
        ],
        0,
    )
    normed = (layer_norm(embedded) * (1.0 + rows_of[1:2]) + rows_of[0:1]).astype(BF16)
    mixed = attention(normed, input_weight[...], output_weight[...], spatial, None)
    after = embedded + rows_of[2:3] * mixed
    for index in range(frames):
        out[at + index] = after[index * spatial : (index + 1) * spatial].astype(out.dtype)


def time_step(at, count, after, rows_of, input_weight, output_weight, final, out, same_position):
    frames, width = after.shape[0], after.shape[2]
    hidden = jnp.concatenate(
        [
            after[:, pl.ds(pl.multiple_of(at + index * ROWS8, ROWS8), ROWS8), :].reshape(
                frames * ROWS8, width
            )
            for index in range(count)
        ],
        0,
    ).astype(F32)
    normed = (layer_norm(hidden) * (1.0 + rows_of[4:5]) + rows_of[3:4]).astype(BF16)
    mixed = attention(
        normed, input_weight[...], output_weight[...], frames * ROWS8, same_position
    )
    settled = hidden + rows_of[5:6] * mixed
    normed = (layer_norm(settled) * (1.0 + rows_of[7:8]) + rows_of[6:7]).astype(BF16)
    predicted = jnp.dot(normed, final[...], preferred_element_type=F32)
    for index in range(count):
        part = predicted[index * frames * ROWS8 : (index + 1) * frames * ROWS8]
        out[:, pl.ds(pl.multiple_of(at + index * ROWS8, ROWS8), ROWS8), :] = part.reshape(
            frames, ROWS8, part.shape[1]
        )


def same_position_mask(frames):
    rows = frames * ROWS8
    row = lax.broadcasted_iota(jnp.int32, (rows, rows), 0) % ROWS8
    column = lax.broadcasted_iota(jnp.int32, (rows, rows), 1) % ROWS8
    return jnp.where(row == column, 1.0, 0.0).astype(F32)


def both(blocks):
    return 2 if blocks % 2 == 0 else 1


def run_space(latent, embed, rows_of, input_weight, output_weight, out):
    frames = latent.shape[0]
    step = both(frames)

    @pl.loop(0, frames // step)
    def _(index):
        space_step(index * step, step, latent, embed, rows_of, input_weight, output_weight, out)


def run_time(after, rows_of, input_weight, output_weight, final, out):
    frames, positions = after.shape[0], after.shape[1]
    step = both(positions // ROWS8)
    same_position = same_position_mask(frames)

    @pl.loop(0, positions // (step * ROWS8))
    def _(index):
        time_step(
            index * step * ROWS8, step, after, rows_of, input_weight, output_weight, final, out,
            same_position,
        )


def fused_kernel(
    latent, rows_of, embed, space_in_hbm, space_out_hbm, time_in_hbm, time_out_hbm, final,
    predicted, space_in, space_out, time_in, time_out, after, staged, sems,
):
    copies = [
        pltpu.make_async_copy(source, target, sems.at[index])
        for index, (source, target) in enumerate(
            (
                (space_in_hbm, space_in),
                (space_out_hbm, space_out),
                (time_in_hbm, time_in),
                (time_out_hbm, time_out),
            )
        )
    ]
    for copy in copies:
        copy.start()
    copies[0].wait()
    copies[1].wait()
    run_space(latent, embed, rows_of, space_in, space_out, after)
    copies[2].wait()
    copies[3].wait()
    run_time(after, rows_of, time_in, time_out, final, staged)
    for frame in range(latent.shape[0]):
        predicted[frame] = staged[frame].T


def space_kernel(latent, rows_of, embed, space_in, space_out, after):
    run_space(latent, embed, rows_of, space_in, space_out, after)


def time_kernel(after, rows_of, time_in, time_out, final, predicted):
    run_time(after, rows_of, time_in, time_out, final, predicted)


def vmem(count):
    return [pl.BlockSpec(memory_space=pltpu.VMEM)] * count


PARAMS = dict(compiler_params=pltpu.CompilerParams(vmem_limit_bytes=56 * 2**20))


def denoise_fused(latent, rows_of, embed, space_in, space_out, time_in, time_out, final):
    frames, channels, spatial = latent.shape
    width = embed.shape[1]
    return pl.pallas_call(
        fused_kernel,
        out_shape=jax.ShapeDtypeStruct(latent.shape, F32),
        in_specs=vmem(3) + [pl.BlockSpec(memory_space=pl.ANY)] * 4 + vmem(1),
        out_specs=vmem(1)[0],
        scratch_shapes=[
            pltpu.VMEM(space_in.shape, BF16),
            pltpu.VMEM(space_out.shape, BF16),
            pltpu.VMEM(time_in.shape, BF16),
            pltpu.VMEM(time_out.shape, BF16),
            pltpu.VMEM((frames, spatial, width), F32),
            pltpu.VMEM((frames, spatial, channels), F32),
            pltpu.SemaphoreType.DMA((4,)),
        ],
        name="denoise",
        **PARAMS,
    )(latent, rows_of, embed, space_in, space_out, time_in, time_out, final)


def denoise_split(latent, rows_of, embed, space_in, space_out, time_in, time_out, final, peers):
    frames, channels, spatial = latent.shape
    width = embed.shape[1]
    after = pl.pallas_call(
        space_kernel,
        out_shape=jax.ShapeDtypeStruct((frames, spatial, width), BF16),
        in_specs=vmem(5),
        out_specs=vmem(1)[0],
        name="space",
        **PARAMS,
    )(latent, rows_of, embed, space_in, space_out)
    after = lax.all_to_all(
        after, "tok", split_axis=1, concat_axis=0, tiled=True, axis_index_groups=peers
    )
    predicted = pl.pallas_call(
        time_kernel,
        out_shape=jax.ShapeDtypeStruct(after.shape[:2] + (channels,), F32),
        in_specs=vmem(5),
        out_specs=vmem(1)[0],
        name="time",
        **PARAMS,
    )(after.astype(F32), rows_of, time_in, time_out, final)
    predicted = lax.all_to_all(
        predicted, "tok", split_axis=0, concat_axis=1, tiled=True, axis_index_groups=peers
    )
    return jnp.swapaxes(predicted, 1, 2)


def sum_before(values, timesteps, groups):
    before = jnp.zeros_like(values)
    reach = 1
    while reach < timesteps:
        moves = [
            (step * groups + block, (step + reach) * groups + block)
            for step in range(timesteps - reach)
            for block in range(groups)
        ]
        held = (values + before).astype(BF16)
        before = before + lax.ppermute(held, "tok", moves).astype(F32)
        reach *= 2
    return before


def body(
    initial_guess,
    noise_draws,
    drift_state,
    drift_denoise,
    noise_scale,
    modulation,
    embed_weight,
    space_input,
    space_output,
    time_input,
    time_output,
    final_weight,
):
    timesteps = modulation.shape[0]
    devices = lax.axis_size("tok")
    groups = devices // timesteps
    timestep = lax.axis_index("tok") // groups
    leading = timestep == 0
    rows_of = lax.dynamic_index_in_dim(modulation, timestep, 0, keepdims=False)
    rate_state = lax.dynamic_index_in_dim(drift_state, timestep, 0, keepdims=False)
    rate_denoise = lax.dynamic_index_in_dim(drift_denoise, timestep, 0, keepdims=False)
    rate_noise = lax.dynamic_index_in_dim(noise_scale, timestep, 0, keepdims=False)
    if groups == 1:
        denoise = denoise_fused
    else:
        peers = [[step * groups + block for block in range(groups)] for step in range(timesteps)]
        denoise = functools.partial(denoise_split, peers=peers)
    weights = (embed_weight, space_input, space_output, time_input, time_output, final_weight)
    latent = initial_guess
    result = initial_guess
    for _ in range(ITERS):
        predicted = denoise(latent, rows_of, *weights)
        increment = rate_state * latent + rate_denoise * predicted + rate_noise * noise_draws
        increment = jnp.where(leading, increment + latent, increment)
        before = sum_before(increment, timesteps, groups)
        result = before + increment
        latent = jnp.where(leading, latent, before)
    return result


def solution(mesh):
    rows = P(("group", "tok"), None, None)
    placed = (rows, rows) + (P(),) * 10
    return jax.shard_map(
        body, mesh=mesh, in_specs=placed, out_specs=rows, check_vma=False
    )
```

time: 744 us -> 238 us (0.32)
  the two profiles are of different devices: /device:TPU:29 before, /device:TPU:0 now
where the time goes in v1:
time: 238 us; the launch traced here: 237 us
  Pallas kernels  157 us (66%)
  starting transfers between devices  41.4 us (17%)
  local copies, waits for them, and re-layouts  19 us (8%)
  waiting for transfers between devices  13 us (5%)
  other arithmetic  7.05 us (3%)
    pallas_call x2, Pallas kernels, denoise_fused(): pl.pallas_call(fused_kernel, out_shape=jax.ShapeDtypeStruct(latent.shape,...  157 us
    ppermute x8, starting transfers between devices, sum_before(): before = before + lax.ppermute(held, 'tok', moves).astype(F32)  41.4 us
    unnamed x11, local copies, waits for them, and re-layouts  14.6 us
    ppermute x8, waiting for transfers between devices, sum_before(): before = before + lax.ppermute(held, 'tok', moves).astype(F32)  13 us
    convert_element_type x8, other arithmetic, sum_before(): held = (values + before).astype(BF16)  5.66 us
  transfers between devices with their start and end apart: 8, of which 8 were waited for; matrix products, arithmetic and copies ran while one was open for 0% of the time, Pallas kernels for 0%

profile of v1, /device:TPU:0, one launch (start us, length us, event | category | flops | bytes accessed | tf_op | source)
XLA Modules:
  0.0 237.1 jit_solution(17241094329518577544)
XLA Ops:
  0.0 0.0 copy-start
  0.0 1.3 dynamic_slice.17
  1.3 1.3 dynamic_slice.15
  2.6 1.2 dynamic_slice.14
  3.8 0.0 copy-done
  3.8 0.6 dynamic-slice_bitcast_fusion.rows_of
  4.4 1.7 copy.15.final
  6.1 6.4 %copy.13.space_in_hbm = bf16[1152,1728]{1,0:T(8,128)(2,1)} copy(bf16[1152,1728]{0,1:T(8,128)(2,1)} %param.19) | data formatting | bytes 7962624 | tf_op args[7]
  12.5 6.4 %copy.14.time_in_hbm = bf16[1152,1728]{1,0:T(8,128)(2,1)} copy(bf16[1152,1728]{0,1:T(8,128)(2,1)} %param.21) | data formatting | bytes 7962624 | tf_op args[9]
  19.0 0.0 copy-start.1
  19.0 0.0 copy-start.3
  19.0 78.3 %denoise.2 = f32[16,16,128]{2,1,0:T(8,128)} custom-call(f32[16,16,128]{2,1,0:T(8,128)} %latent.1, f32[8,1152]{1,0:T(8,128)} %dynamic-slice_bitcast_fusion.rows_of, bf16[16,1152]{1,0:T(8,128)(2,1)} %embed.3, bf16[1152,1728]{1,0:T(8,128)(2,1)} %copy.13.space_in_hbm, bf16[576,1152]{1,0:T(8,128)(2,1)} %space_out_hbm.3, bf16[1152,1728]{1,0:T(8,128)(2,1)} %copy.14.time_in_hbm, ...), custom_call_target="tpu_custom_call" | custom-call | tf_op jit(solution)/shard_map/denoise/pallas_call | solution.py:250
  97.3 0.0 copy-done.1
  97.3 0.0 copy-done.3
  97.3 2.8 %fusion.3 = (bf16[16,16,128]{2,1,0:T(8,128)(2,1)S(1)}, f32[16,16,128]{2,1,0:T(8,128)S(1)}) fusion(f32[16,16,128]{2,1,0:T(8,128)S(1)} %copy-done.1, f32[16,16,128]{2,1,0:T(8,128)S(1)} %copy-done.3, f32[]{:T(128)} %bitcast.3, f32[16,16,128]{2,1,0:T(8,128)} %denoise.2, f32[]{:T(128)} %bitcast.1, f32[]{:T(128)} %bitcast, pred[]{:T(512)S(6)} %eq.3), kind=kLoop, calls=%fused_computation.18 | loop fusion | flops 262144 | bytes 589837 | tf_op jit(solution)/shard_map/convert_element_type | solution.py:306
  100.1 2.4 collective-permute-start
  102.4 0.9 collective-permute-done
  103.3 7.2 %collective-permute-start.1 = (bf16[16,16,128]{2,1,0:T(8,128)(2,1)S(1)}, bf16[16,16,128]{2,1,0:T(8,128)(2,1)S(1)}, u32[]{:S(2)}, u32[]{:S(2)}) collective-permute-start(bf16[16,16,128]{2,1,0:T(8,128)(2,1)S(1)} %fusion), channel_id=1, source_target_pairs={{0,2},{1,3},{2,4},{3,5},{4,6},{5,7},{6,8},{7,9},{8,10},{9,11},{10,... | collective-permute-start | bytes 196616 | tf_op jit(solution)/shard_map/ppermute | solution.py:307
  110.5 1.9 collective-permute-done.1
  112.5 6.1 %collective-permute-start.2 = (bf16[16,16,128]{2,1,0:T(8,128)(2,1)S(1)}, bf16[16,16,128]{2,1,0:T(8,128)(2,1)S(1)}, u32[]{:S(2)}, u32[]{:S(2)}) collective-permute-start(bf16[16,16,128]{2,1,0:T(8,128)(2,1)S(1)} %add_convert_fusion.3), channel_id=1, source_target_pairs={{0,4},{1,5},{2,6},{3,7},{4,8},{5,9},{6,10},{7,11},{8,12},{9,13},{1... | collective-permute-start | bytes 196616 | tf_op jit(solution)/shard_map/ppermute | solution.py:307
  118.6 1.9 collective-permute-done.2
  120.5 5.5 %collective-permute-start.3 = (bf16[16,16,128]{2,1,0:T(8,128)(2,1)S(1)}, bf16[16,16,128]{2,1,0:T(8,128)(2,1)S(1)}, u32[]{:S(2)}, u32[]{:S(2)}) collective-permute-start(bf16[16,16,128]{2,1,0:T(8,128)(2,1)S(1)} %add_convert_fusion.2), channel_id=1, source_target_pairs={{0,8},{1,9},{2,10},{3,11},{4,12},{5,13},{6,14},{7,15},{16,24},{17,... | collective-permute-start | bytes 196616 | tf_op jit(solution)/shard_map/ppermute | solution.py:307
  126.0 1.7 collective-permute-done.3
  127.7 0.7 add_select_fusion.2.latent
  128.4 0.0 copy-start.2
  128.4 78.3 %denoise.3 = f32[16,16,128]{2,1,0:T(8,128)} custom-call(f32[16,16,128]{2,1,0:T(8,128)} %add_select_fusion.2.latent, f32[8,1152]{1,0:T(8,128)} %dynamic-slice_bitcast_fusion.rows_of, bf16[16,1152]{1,0:T(8,128)(2,1)} %embed.3, bf16[1152,1728]{1,0:T(8,128)(2,1)} %copy.13.space_in_hbm, bf16[576,1152]{1,0:T(8,128)(2,1)} %space_out_hbm.3, ...), custom_call_target="tpu_custom_call" | custom-call | tf_op jit(solution)/shard_map/denoise/pallas_call | solution.py:250
  206.7 0.0 copy-done.2
  206.7 2.8 %fusion.2 = (bf16[16,16,128]{2,1,0:T(8,128)(2,1)S(1)}, f32[16,16,128]{2,1,0:T(8,128)S(1)}) fusion(f32[16,16,128]{2,1,0:T(8,128)S(1)} %copy-done.2, f32[16,16,128]{2,1,0:T(8,128)S(1)} %copy-done.3, f32[]{:T(128)} %bitcast.3, f32[16,16,128]{2,1,0:T(8,128)} %denoise.3, f32[]{:T(128)} %bitcast.1, f32[]{:T(128)} %bitcast, pred[]{:T(512)S(6)} %eq.3), kind=kLoop, calls=%fused_computation.17 | loop fusion | flops 262144 | bytes 589837 | tf_op jit(solution)/shard_map/convert_element_type | solution.py:306
  209.4 1.3 collective-permute-start.4
  210.7 0.9 collective-permute-done.4
  211.6 5.1 %collective-permute-start.5 = (bf16[16,16,128]{2,1,0:T(8,128)(2,1)S(1)}, bf16[16,16,128]{2,1,0:T(8,128)(2,1)S(1)}, u32[]{:S(2)}, u32[]{:S(2)}) collective-permute-start(bf16[16,16,128]{2,1,0:T(8,128)(2,1)S(1)} %fusion.1), channel_id=1, source_target_pairs={{0,2},{1,3},{2,4},{3,5},{4,6},{5,7},{6,8},{7,9},{8,10},{9,11},{10,... | collective-permute-start | bytes 196616 | tf_op jit(solution)/shard_map/ppermute | solution.py:307
  216.8 2.0 collective-permute-done.5
  218.8 8.2 %collective-permute-start.6 = (bf16[16,16,128]{2,1,0:T(8,128)(2,1)S(1)}, bf16[16,16,128]{2,1,0:T(8,128)(2,1)S(1)}, u32[]{:S(2)}, u32[]{:S(2)}) collective-permute-start(bf16[16,16,128]{2,1,0:T(8,128)(2,1)S(1)} %add_convert_fusion.1), channel_id=1, source_target_pairs={{0,4},{1,5},{2,6},{3,7},{4,8},{5,9},{6,10},{7,11},{8,12},{9,13},{1... | collective-permute-start | bytes 196616 | tf_op jit(solution)/shard_map/ppermute | solution.py:307
  227.0 1.9 collective-permute-done.6
  228.9 5.6 %collective-permute-start.7 = (bf16[16,16,128]{2,1,0:T(8,128)(2,1)S(1)}, bf16[16,16,128]{2,1,0:T(8,128)(2,1)S(1)}, u32[]{:S(2)}, u32[]{:S(2)}) collective-permute-start(bf16[16,16,128]{2,1,0:T(8,128)(2,1)S(1)} %add_convert_fusion), channel_id=1, source_target_pairs={{0,8},{1,9},{2,10},{3,11},{4,12},{5,13},{6,14},{7,15},{16,24},{17,... | collective-permute-start | bytes 196616 | tf_op jit(solution)/shard_map/ppermute | solution.py:307
  234.5 1.9 collective-permute-done.7
  236.4 0.7 add_add_fusion
  (6 shorter events, 0.2 us)
Async XLA Ops:
  0.0 3.8 %copy-start = (f32[16,8,1152]{2,1,0:T(8,128)S(1)}, f32[16,8,1152]{2,1,0:T(8,128)}, u32[]{:S(2)}) copy-start(f32[16,8,1152]{2,1,0:T(8,128)} %param.17) | copy-start | bytes 1769476
  19.0 78.3 %copy-start.1 = (f32[16,16,128]{2,1,0:T(8,128)S(1)}, f32[16,16,128]{2,1,0:T(8,128)}, u32[]{:S(2)}) copy-start(f32[16,16,128]{2,1,0:T(8,128)} %latent.1) | copy-start | bytes 393220
  19.0 78.3 %copy-start.3 = (f32[16,16,128]{2,1,0:T(8,128)S(1)}, f32[16,16,128]{2,1,0:T(8,128)}, u32[]{:S(2)}) copy-start(f32[16,16,128]{2,1,0:T(8,128)} %param.13) | copy-start | bytes 393220
  100.1 3.3 %collective-permute-start = (bf16[16,16,128]{2,1,0:T(8,128)(2,1)S(1)}, bf16[16,16,128]{2,1,0:T(8,128)(2,1)S(1)}, u32[]{:S(2)}, u32[]{:S(2)}) collective-permute-start(bf16[16,16,128]{2,1,0:T(8,128)(2,1)S(1)} %get-tuple-element.7), channel_id=1, source_target_pairs={{0,1},{1,2},{2,3},{3,4},{4,5},{5,6},{6,7},{7,8},{8,9},{9,10},{10,1... | collective-permute-start | bytes 196616 | tf_op jit(solution)/shard_map/ppermute | solution.py:307
  103.3 9.1 %collective-permute-start.1 = (bf16[16,16,128]{2,1,0:T(8,128)(2,1)S(1)}, bf16[16,16,128]{2,1,0:T(8,128)(2,1)S(1)}, u32[]{:S(2)}, u32[]{:S(2)}) collective-permute-start(bf16[16,16,128]{2,1,0:T(8,128)(2,1)S(1)} %fusion), channel_id=1, source_target_pairs={{0,2},{1,3},{2,4},{3,5},{4,6},{5,7},{6,8},{7,9},{8,10},{9,11},{10,... | collective-permute-start | bytes 196616 | tf_op jit(solution)/shard_map/ppermute | solution.py:307
  112.5 8.0 %collective-permute-start.2 = (bf16[16,16,128]{2,1,0:T(8,128)(2,1)S(1)}, bf16[16,16,128]{2,1,0:T(8,128)(2,1)S(1)}, u32[]{:S(2)}, u32[]{:S(2)}) collective-permute-start(bf16[16,16,128]{2,1,0:T(8,128)(2,1)S(1)} %add_convert_fusion.3), channel_id=1, source_target_pairs={{0,4},{1,5},{2,6},{3,7},{4,8},{5,9},{6,10},{7,11},{8,12},{9,13},{1... | collective-permute-start | bytes 196616 | tf_op jit(solution)/shard_map/ppermute | solution.py:307
  120.5 7.2 %collective-permute-start.3 = (bf16[16,16,128]{2,1,0:T(8,128)(2,1)S(1)}, bf16[16,16,128]{2,1,0:T(8,128)(2,1)S(1)}, u32[]{:S(2)}, u32[]{:S(2)}) collective-permute-start(bf16[16,16,128]{2,1,0:T(8,128)(2,1)S(1)} %add_convert_fusion.2), channel_id=1, source_target_pairs={{0,8},{1,9},{2,10},{3,11},{4,12},{5,13},{6,14},{7,15},{16,24},{17,... | collective-permute-start | bytes 196616 | tf_op jit(solution)/shard_map/ppermute | solution.py:307
  128.4 78.3 %copy-start.2 = (f32[16,16,128]{2,1,0:T(8,128)S(1)}, f32[16,16,128]{2,1,0:T(8,128)}, u32[]{:S(2)}) copy-start(f32[16,16,128]{2,1,0:T(8,128)} %add_select_fusion.2.latent) | copy-start | bytes 393220
  209.4 2.2 collective-permute-start.4
  211.6 7.1 %collective-permute-start.5 = (bf16[16,16,128]{2,1,0:T(8,128)(2,1)S(1)}, bf16[16,16,128]{2,1,0:T(8,128)(2,1)S(1)}, u32[]{:S(2)}, u32[]{:S(2)}) collective-permute-start(bf16[16,16,128]{2,1,0:T(8,128)(2,1)S(1)} %fusion.1), channel_id=1, source_target_pairs={{0,2},{1,3},{2,4},{3,5},{4,6},{5,7},{6,8},{7,9},{8,10},{9,11},{10,... | collective-permute-start | bytes 196616 | tf_op jit(solution)/shard_map/ppermute | solution.py:307
  218.8 10.1 %collective-permute-start.6 = (bf16[16,16,128]{2,1,0:T(8,128)(2,1)S(1)}, bf16[16,16,128]{2,1,0:T(8,128)(2,1)S(1)}, u32[]{:S(2)}, u32[]{:S(2)}) collective-permute-start(bf16[16,16,128]{2,1,0:T(8,128)(2,1)S(1)} %add_convert_fusion.1), channel_id=1, source_target_pairs={{0,4},{1,5},{2,6},{3,7},{4,8},{5,9},{6,10},{7,11},{8,12},{9,13},{1... | collective-permute-start | bytes 196616 | tf_op jit(solution)/shard_map/ppermute | solution.py:307
  228.9 7.5 %collective-permute-start.7 = (bf16[16,16,128]{2,1,0:T(8,128)(2,1)S(1)}, bf16[16,16,128]{2,1,0:T(8,128)(2,1)S(1)}, u32[]{:S(2)}, u32[]{:S(2)}) collective-permute-start(bf16[16,16,128]{2,1,0:T(8,128)(2,1)S(1)} %add_convert_fusion), channel_id=1, source_target_pairs={{0,8},{1,9},{2,10},{3,11},{4,12},{5,13},{6,14},{7,15},{16,24},{17,... | collective-permute-start | bytes 196616 | tf_op jit(solution)/shard_map/ppermute | solution.py:307
